TPU v7x, 32 devices: a whole 2x2x4 slice. The times are simulated.
32 devices in a mesh: build: 8 (over y, x, core), lat: 4 (over z).
Axes of the slice: x: 2, y: 2, z: 4, core: 2. Of those that a mesh axis runs over, the one named last changes fastest.
Arguments:
- density: float32 [16, 64, 1024], P('build', 'lat'), may hold values from 0.03 to 1
- support_mask: int32 [64, 1024], P('lat'), may hold values from 0 to 1
- pattern: int32 [27], replicated, may hold values from 0 to 7
- blocks: float32 [8, 3, 3], replicated, may hold values from -0.625 to 0.625
- displacement: float32 [3, 16, 64, 1024], P(None, 'build', 'lat'), may hold values from -6 to 6
- adjoint: float32 [3, 16, 64, 1024], P(None, 'build', 'lat'), may hold values from -6 to 6
Outputs:
- force: float32 [3, 16, 64, 1024], P(None, 'build', 'lat')
- sensitivity: float32 [16, 64, 1024], P('build', 'lat')
All inputs are finite; a program needn't handle non-finite values.
Results may differ from a plain program's by a relative error of at most 0.0003.
Values sent between devices are 32-bit elements; how exact they have to be, the bound alone decides.
A program may use at most 64 MiB of HBM per device.

v0:
```python
import jax
import jax.numpy as jnp
from jax import lax
from jax.sharding import PartitionSpec as P

exponent = 16.0
smooth_eps = 0.0001
root_eps = 0.01
base_floor = 0.05
modulus_floor = 0.001
highest = lax.Precision.HIGHEST


def extended(shard, sides, width):
    for axis, dim in sides:
        devices, length = (lax.axis_size(axis), shard.shape[dim])
        up = [(i, (i + 1) % devices) for i in range(devices - 1)]
        down = [(j, i) for i, j in up]
        last = lax.slice_in_dim(shard, length - width, length, axis=dim)
        initial = lax.slice_in_dim(shard, 0, width, axis=dim)
        before = lax.ppermute(last, axis, up)
        after = lax.ppermute(initial, axis, down)
        shard = jnp.concatenate([before, shard, after], axis=dim)
    return shard


def from_behind(block, axis, distance):
    devices = range(lax.axis_size(axis))
    route = [(i - distance, i) for i in devices if i - distance in devices]
    return lax.ppermute(block, axis, route)


def cross_local(padded):
    centre = padded[1:-1]
    widened = jnp.pad(centre, ((0, 0), (1, 1)))
    return centre + padded[:-2] + padded[2:] + widened[:, :-2] + widened[:, 2:]


def forward_block(design, bottom, inside):

    def forward_layer(from_below, design_layer):
        padded = extended(from_below**exponent, (("lat", 0),), 1)
        support = cross_local(padded) ** (1.0 / exponent)
        differ = design_layer - support
        printed = (
            0.5
            * (design_layer + support - jnp.sqrt(differ * differ + smooth_eps) + root_eps)
            * inside
        )
        return (printed, (printed, support))

    _, (printed, support) = lax.scan(forward_layer, bottom, design)
    return (printed, support)


def backward_block(direct, printed, support, design, incoming, inside):
    safe_support = jnp.where(inside > 0.5, support, 1.0)

    def backward_layer(from_above, layer_items):
        direct_layer, printed_layer, support_layer, design_layer = layer_items
        padded = extended(from_above, (("lat", 0),), 1)
        weight_total = direct_layer + printed_layer ** (exponent - 1.0) * cross_local(padded)
        differ = design_layer - support_layer
        slope_term = differ / jnp.sqrt(differ * differ + smooth_eps)
        sensitivity = weight_total * 0.5 * (1.0 - slope_term)
        passed = (
            weight_total * 0.5 * (1.0 + slope_term) / support_layer ** (exponent - 1.0) * inside
        )
        return (passed, sensitivity)

    outgoing, sensitivity = lax.scan(
        backward_layer, incoming, (direct, printed, safe_support, design), reverse=True
    )
    return (sensitivity, outgoing)


def whole_forward(density, base_plane, position, build_count):
    inside = jnp.ones((density.shape[2],), jnp.float32)
    zero_block = jnp.zeros(density.shape, jnp.float32)

    def forward_section(section_number, carried):
        received = from_behind(carried[0][-1], "build", 1)
        bottom = jnp.where(position == 0, base_plane, received)
        return forward_block(density, bottom, inside)

    return lax.fori_loop(0, build_count, forward_section, (zero_block, zero_block))


def whole_backward(direct, printed, support, density, build_count):
    inside = jnp.ones((density.shape[2],), jnp.float32)
    zero_block = jnp.zeros(density.shape, jnp.float32)
    zero_plane = jnp.zeros(density.shape[1:], jnp.float32)

    def backward_section(section_number, carried):
        received = from_behind(carried[1], "build", -1)
        return backward_block(direct, printed, support, density, received, inside)

    sensitivity, _ = lax.fori_loop(0, build_count, backward_section, (zero_block, zero_plane))
    return sensitivity


def apply_blocks(rimmed, blocks_used, reverse):
    widened = jnp.pad(rimmed, ((0, 0), (0, 0), (0, 0), (1, 1)))
    layer_count = rimmed.shape[1] - 2
    width_x = rimmed.shape[2] - 2
    width_y = rimmed.shape[3]
    result = jnp.zeros((rimmed.shape[0], layer_count, width_x, width_y), jnp.float32)
    direction = -1 if reverse else 1
    number = 0
    for step_z in (-1, 0, 1):
        for step_x in (-1, 0, 1):
            for step_y in (-1, 0, 1):
                start_z = 1 + direction * step_z
                start_x = 1 + direction * step_x
                start_y = 1 + direction * step_y
                shifted = widened[
                    :,
                    start_z : start_z + layer_count,
                    start_x : start_x + width_x,
                    start_y : start_y + width_y,
                ]
                matrix = blocks_used[number].T if reverse else blocks_used[number]
                result = result + jnp.einsum("cd,dzxy->czxy", matrix, shifted, precision=highest)
                number += 1
    return result


def on_device(density, support_mask, pattern, blocks, displacement, adjoint):
    build_count = lax.axis_size("build")
    position = lax.axis_index("build")
    early_rims = extended(
        jnp.concatenate([displacement, adjoint], 0), (("build", 1), ("lat", 2)), 1
    )
    base_plane = base_floor + (1.0 - base_floor) * support_mask.astype(jnp.float32)
    printed, support = whole_forward(density, base_plane, position, build_count)
    modulus = modulus_floor + (1.0 - modulus_floor) * printed**3
    table_rows = blocks.shape[0]
    onehot = (pattern[:, None] == jnp.arange(table_rows, dtype=jnp.int32)[None, :]).astype(
        jnp.float32
    )
    blocks_used = jnp.dot(onehot, blocks.reshape(table_rows, 9), precision=highest).reshape(
        27, 3, 3
    )
    moduli = extended(modulus, (("build", 0), ("lat", 1)), 1)
    loaded = moduli[None] * early_rims[:3]
    pulled_in = early_rims[3:]
    force = apply_blocks(loaded, blocks_used, False)
    pulled = apply_blocks(pulled_in, blocks_used, True)
    direct = jnp.sum(displacement * pulled, axis=0) * (3.0 * (1.0 - modulus_floor)) * printed**2
    sensitivity = whole_backward(direct, printed, support, density, build_count)
    return (force, sensitivity)


def solution(mesh):
    in_specs = (
        P("build", "lat", None),
        P("lat", None),
        P(),
        P(),
        P(None, "build", "lat", None),
        P(None, "build", "lat", None),
    )
    out_specs = (P(None, "build", "lat", None), P("build", "lat", None))
    return jax.shard_map(
        on_device, mesh=mesh, in_specs=in_specs, out_specs=out_specs, check_vma=False
    )
```

profile of v0, /device:TPU:28, one launch (start us, length us, event | category | flops | bytes accessed | tf_op | source)
XLA Modules:
  0.0 457.0 jit_solution(2693231403718886171)
XLA Ops:
  5.4 4.5 collective-permute-start.11
  10.7 183.4 %while.77 = (s32[]{:T(128)}, f32[2,16,1024]{2,1,0:T(8,128)S(1)}, f32[2,16,1024]{2,1,0:T(8,128)}, pred[]{:T(512)}, f32[16,1024]{1,0:T(8,128)S(1)}, /*index=5*/f32...) while((s32[]{:T(128)}, f32[2,16,1024]{2,1,0:T(8,128)S(1)}, ...), condition=%wide.region_3.4_spmd, body=%wide.region_0.3_spmd.sunk | while | flops 229380 | bytes 1761671 | solution.py:86
  12.8 6.5 %collective-permute-done.5 = f32[16,1024]{1,0:T(8,128)S(1)} collective-permute-done((f32[16,1024]{1,0:T(8,128)S(1)}, f32[16,1024]{1,0:T(8,128)S(1)}, u32[]{:S(2)}, u32[]{:S(2)}) %collective-permute-start.5) | collective-permute-done | bytes 65568 | tf_op jit(solution)/shard_map/while/body/eval_jaxpr/ppermute | solution.py:30
  19.3 16.2 %while.80 = (s32[]{:T(128)}, f32[16,1024]{1,0:T(8,128)S(1)}, f32[2,16,1024]{2,1,0:T(8,128)S(1)}, f32[2,16,1024]{2,1,0:T(8,128)S(1)}, f32[2,16,1024]{2,1,0:T(8,128)S(1)}, /*index=5*/s32[]{:T(128)}) while((s32[]{:T(128)}, f32[16,1024]{1,0:T(8,128)S(1)}, f32[2,16,1024]{2,1,0:T(8,128)S(1)}, f32[2,16,1024]{2,1,0:T(8,128)S(1)}, ...), condition=%wide.region_2.2_spmd, body=%wide.region_1.1_spmd.sunk | while | flops 212994 | bytes 647333 | solution.py:52
  38.1 4.5 collective-permute-done.5
  42.7 15.8 %while.80 = (s32[]{:T(128)}, f32[16,1024]{1,0:T(8,128)S(1)}, f32[2,16,1024]{2,1,0:T(8,128)S(1)}, f32[2,16,1024]{2,1,0:T(8,128)S(1)}, f32[2,16,1024]{2,1,0:T(8,128)S(1)}, /*index=5*/s32[]{:T(128)}) while((s32[]{:T(128)}, f32[16,1024]{1,0:T(8,128)S(1)}, f32[2,16,1024]{2,1,0:T(8,128)S(1)}, f32[2,16,1024]{2,1,0:T(8,128)S(1)}, ...), condition=%wide.region_2.2_spmd, body=%wide.region_1.1_spmd.sunk | while | flops 212994 | bytes 647333 | solution.py:52
  65.6 15.3 %while.80 = (s32[]{:T(128)}, f32[16,1024]{1,0:T(8,128)S(1)}, f32[2,16,1024]{2,1,0:T(8,128)S(1)}, f32[2,16,1024]{2,1,0:T(8,128)S(1)}, f32[2,16,1024]{2,1,0:T(8,128)S(1)}, /*index=5*/s32[]{:T(128)}) while((s32[]{:T(128)}, f32[16,1024]{1,0:T(8,128)S(1)}, f32[2,16,1024]{2,1,0:T(8,128)S(1)}, f32[2,16,1024]{2,1,0:T(8,128)S(1)}, ...), condition=%wide.region_2.2_spmd, body=%wide.region_1.1_spmd.sunk | while | flops 212994 | bytes 647333 | solution.py:52
  88.1 15.3 %while.80 = (s32[]{:T(128)}, f32[16,1024]{1,0:T(8,128)S(1)}, f32[2,16,1024]{2,1,0:T(8,128)S(1)}, f32[2,16,1024]{2,1,0:T(8,128)S(1)}, f32[2,16,1024]{2,1,0:T(8,128)S(1)}, /*index=5*/s32[]{:T(128)}) while((s32[]{:T(128)}, f32[16,1024]{1,0:T(8,128)S(1)}, f32[2,16,1024]{2,1,0:T(8,128)S(1)}, f32[2,16,1024]{2,1,0:T(8,128)S(1)}, ...), condition=%wide.region_2.2_spmd, body=%wide.region_1.1_spmd.sunk | while | flops 212994 | bytes 647333 | solution.py:52
  110.6 15.3 %while.80 = (s32[]{:T(128)}, f32[16,1024]{1,0:T(8,128)S(1)}, f32[2,16,1024]{2,1,0:T(8,128)S(1)}, f32[2,16,1024]{2,1,0:T(8,128)S(1)}, f32[2,16,1024]{2,1,0:T(8,128)S(1)}, /*index=5*/s32[]{:T(128)}) while((s32[]{:T(128)}, f32[16,1024]{1,0:T(8,128)S(1)}, f32[2,16,1024]{2,1,0:T(8,128)S(1)}, f32[2,16,1024]{2,1,0:T(8,128)S(1)}, ...), condition=%wide.region_2.2_spmd, body=%wide.region_1.1_spmd.sunk | while | flops 212994 | bytes 647333 | solution.py:52
  133.1 15.3 %while.80 = (s32[]{:T(128)}, f32[16,1024]{1,0:T(8,128)S(1)}, f32[2,16,1024]{2,1,0:T(8,128)S(1)}, f32[2,16,1024]{2,1,0:T(8,128)S(1)}, f32[2,16,1024]{2,1,0:T(8,128)S(1)}, /*index=5*/s32[]{:T(128)}) while((s32[]{:T(128)}, f32[16,1024]{1,0:T(8,128)S(1)}, f32[2,16,1024]{2,1,0:T(8,128)S(1)}, f32[2,16,1024]{2,1,0:T(8,128)S(1)}, ...), condition=%wide.region_2.2_spmd, body=%wide.region_1.1_spmd.sunk | while | flops 212994 | bytes 647333 | solution.py:52
  155.6 15.3 %while.80 = (s32[]{:T(128)}, f32[16,1024]{1,0:T(8,128)S(1)}, f32[2,16,1024]{2,1,0:T(8,128)S(1)}, f32[2,16,1024]{2,1,0:T(8,128)S(1)}, f32[2,16,1024]{2,1,0:T(8,128)S(1)}, /*index=5*/s32[]{:T(128)}) while((s32[]{:T(128)}, f32[16,1024]{1,0:T(8,128)S(1)}, f32[2,16,1024]{2,1,0:T(8,128)S(1)}, f32[2,16,1024]{2,1,0:T(8,128)S(1)}, ...), condition=%wide.region_2.2_spmd, body=%wide.region_1.1_spmd.sunk | while | flops 212994 | bytes 647333 | solution.py:52
  178.1 15.3 %while.80 = (s32[]{:T(128)}, f32[16,1024]{1,0:T(8,128)S(1)}, f32[2,16,1024]{2,1,0:T(8,128)S(1)}, f32[2,16,1024]{2,1,0:T(8,128)S(1)}, f32[2,16,1024]{2,1,0:T(8,128)S(1)}, /*index=5*/s32[]{:T(128)}) while((s32[]{:T(128)}, f32[16,1024]{1,0:T(8,128)S(1)}, f32[2,16,1024]{2,1,0:T(8,128)S(1)}, f32[2,16,1024]{2,1,0:T(8,128)S(1)}, ...), condition=%wide.region_2.2_spmd, body=%wide.region_1.1_spmd.sunk | while | flops 212994 | bytes 647333 | solution.py:52
  196.0 4.5 collective-permute-start.7
  207.5 4.5 collective-permute-start.9
  213.4 4.7 %collective-permute-start.13 = (f32[6,4,1,1024]{3,0,2,1:T(8,128)S(1)}, f32[6,4,1,1024]{3,0,2,1:T(8,128)S(1)}, u32[]{:S(2)}, u32[]{:S(2)}) collective-permute-start(f32[6,4,1,1024]{3,0,2,1:T(8,128)S(1)} %get-tuple-element.567), channel_id=1, source_target_pairs={{1,0},{2,1},{3,2},{5,4},{6,5},{7,6},{9,8},{10,9},{11,10},{13,12},{... | collective-permute-start | bytes 294920 | tf_op jit(solution)/shard_map/ppermute | solution.py:22
  293.5 163.0 %while.79 = (s32[]{:T(128)}, f32[2,16,1024]{2,1,0:T(8,128)}, f32[16,1024]{1,0:T(8,128)S(1)}, f32[2,16,1024]{2,1,0:T(8,128)S(1)}, f32[2,16,1024]{2,1,0:T(8,128)S(...) while((s32[]{:T(128)}, f32[2,16,1024]{2,1,0:T(8,128)}, ...), condition=%wide.region_8.9_spmd, body=%wide.region_5.8_spmd.sunk | while | flops 360453 | bytes 1827262 | solution.py:98
  297.4 17.7 %while.81 = (s32[]{:T(128)}, f32[16,1024]{1,0:T(8,128)S(1)}, f32[2,16,1024]{2,1,0:T(8,128)S(1)}, f32[2,16,1024]{2,1,0:T(8,128)S(1)}, f32[2,16,1024]{2,1,0:T(8,12...) while((s32[]{:T(128)}, f32[16,1024]{1,0:T(8,128)S(1)}, ...), condition=%wide.region_7.7_spmd, body=%wide.region_6.6_spmd.sunk | while | flops 360451 | bytes 778425 | solution.py:71
  319.6 15.6 %while.81 = (s32[]{:T(128)}, f32[16,1024]{1,0:T(8,128)S(1)}, f32[2,16,1024]{2,1,0:T(8,128)S(1)}, f32[2,16,1024]{2,1,0:T(8,128)S(1)}, f32[2,16,1024]{2,1,0:T(8,12...) while((s32[]{:T(128)}, f32[16,1024]{1,0:T(8,128)S(1)}, ...), condition=%wide.region_7.7_spmd, body=%wide.region_6.6_spmd.sunk | while | flops 360451 | bytes 778425 | solution.py:71
  339.7 15.6 %while.81 = (s32[]{:T(128)}, f32[16,1024]{1,0:T(8,128)S(1)}, f32[2,16,1024]{2,1,0:T(8,128)S(1)}, f32[2,16,1024]{2,1,0:T(8,128)S(1)}, f32[2,16,1024]{2,1,0:T(8,12...) while((s32[]{:T(128)}, f32[16,1024]{1,0:T(8,128)S(1)}, ...), condition=%wide.region_7.7_spmd, body=%wide.region_6.6_spmd.sunk | while | flops 360451 | bytes 778425 | solution.py:71
  359.9 15.6 %while.81 = (s32[]{:T(128)}, f32[16,1024]{1,0:T(8,128)S(1)}, f32[2,16,1024]{2,1,0:T(8,128)S(1)}, f32[2,16,1024]{2,1,0:T(8,128)S(1)}, f32[2,16,1024]{2,1,0:T(8,12...) while((s32[]{:T(128)}, f32[16,1024]{1,0:T(8,128)S(1)}, ...), condition=%wide.region_7.7_spmd, body=%wide.region_6.6_spmd.sunk | while | flops 360451 | bytes 778425 | solution.py:71
  380.0 15.6 %while.81 = (s32[]{:T(128)}, f32[16,1024]{1,0:T(8,128)S(1)}, f32[2,16,1024]{2,1,0:T(8,128)S(1)}, f32[2,16,1024]{2,1,0:T(8,128)S(1)}, f32[2,16,1024]{2,1,0:T(8,12...) while((s32[]{:T(128)}, f32[16,1024]{1,0:T(8,128)S(1)}, ...), condition=%wide.region_7.7_spmd, body=%wide.region_6.6_spmd.sunk | while | flops 360451 | bytes 778425 | solution.py:71
  400.1 15.6 %while.81 = (s32[]{:T(128)}, f32[16,1024]{1,0:T(8,128)S(1)}, f32[2,16,1024]{2,1,0:T(8,128)S(1)}, f32[2,16,1024]{2,1,0:T(8,128)S(1)}, f32[2,16,1024]{2,1,0:T(8,12...) while((s32[]{:T(128)}, f32[16,1024]{1,0:T(8,128)S(1)}, ...), condition=%wide.region_7.7_spmd, body=%wide.region_6.6_spmd.sunk | while | flops 360451 | bytes 778425 | solution.py:71
  420.2 15.6 %while.81 = (s32[]{:T(128)}, f32[16,1024]{1,0:T(8,128)S(1)}, f32[2,16,1024]{2,1,0:T(8,128)S(1)}, f32[2,16,1024]{2,1,0:T(8,128)S(1)}, f32[2,16,1024]{2,1,0:T(8,12...) while((s32[]{:T(128)}, f32[16,1024]{1,0:T(8,128)S(1)}, ...), condition=%wide.region_7.7_spmd, body=%wide.region_6.6_spmd.sunk | while | flops 360451 | bytes 778425 | solution.py:71
  440.3 15.6 %while.81 = (s32[]{:T(128)}, f32[16,1024]{1,0:T(8,128)S(1)}, f32[2,16,1024]{2,1,0:T(8,128)S(1)}, f32[2,16,1024]{2,1,0:T(8,128)S(1)}, f32[2,16,1024]{2,1,0:T(8,12...) while((s32[]{:T(128)}, f32[16,1024]{1,0:T(8,128)S(1)}, ...), condition=%wide.region_7.7_spmd, body=%wide.region_6.6_spmd.sunk | while | flops 360451 | bytes 778425 | solution.py:71
  (503 shorter events, 423.3 us)
Async XLA Ops:
  3.5 208.6 %collective-permute-start.10 = (f32[6,1,16,1024]{3,0,2,1:T(8,128)}, f32[6,1,16,1024]{3,0,2,1:T(8,128)S(1)}, u32[]{:S(2)}, u32[]{:S(2)}) collective-permute-start(f32[6,1,16,1024]{3,0,2,1:T(8,128)} %get-tuple-element.568), channel_id=1, source_target_pairs={{0,4},{4,8},{8,12},{12,16},{16,20},{20,24},{24,28},{1,5},{5,9},{9,... | collective-permute-start | bytes 1179656 | tf_op jit(solution)/shard_map/ppermute | solution.py:21
  5.4 206.6 %collective-permute-start.11 = (f32[6,1,16,1024]{3,0,2,1:T(8,128)}, f32[6,1,16,1024]{3,0,2,1:T(8,128)S(1)}, u32[]{:S(2)}, u32[]{:S(2)}) collective-permute-start(f32[6,1,16,1024]{3,0,2,1:T(8,128)} %get-tuple-element.569), channel_id=1, source_target_pairs={{4,0},{8,4},{12,8},{16,12},{20,16},{24,20},{28,24},{5,1},{9,5},{13... | collective-permute-start | bytes 1179656 | tf_op jit(solution)/shard_map/ppermute | solution.py:22
  10.7 8.6 %collective-permute-start.5 = (f32[16,1024]{1,0:T(8,128)S(1)}, f32[16,1024]{1,0:T(8,128)S(1)}, u32[]{:S(2)}, u32[]{:S(2)}) collective-permute-start(f32[16,1024]{1,0:T(8,128)S(1)} %slice_bitcast_fusion.2), channel_id=1, source_target_pairs={{0,4},{4,8},{8,12},{12,16},{16,20},{20,24},{24,28},{1,5},{5,9},{9,... | collective-permute-start | bytes 196616 | tf_op jit(solution)/shard_map/while/body/eval_jaxpr/ppermute | solution.py:30
  21.7 5.5 %collective-permute-start.4 = (f32[1,1024]{1,0:T(1,128)S(1)}, f32[1,1024]{1,0:T(1,128)S(1)}, u32[]{:S(2)}, u32[]{:S(2)}) collective-permute-start(f32[1,1024]{1,0:T(1,128)S(1)} %get-tuple-element.773), channel_id=1, source_target_pairs={{0,1},{1,2},{2,3},{4,5},{5,6},{6,7},{8,9},{9,10},{10,11},{12,13},{... | collective-permute-start | bytes 12296 | tf_op jit(solution)/shard_map/while/body/eval_jaxpr/while/body/eval_jaxpr/ppermute | solution.py:21
  29.9 5.5 %collective-permute-start.4 = (f32[1,1024]{1,0:T(1,128)S(1)}, f32[1,1024]{1,0:T(1,128)S(1)}, u32[]{:S(2)}, u32[]{:S(2)}) collective-permute-start(f32[1,1024]{1,0:T(1,128)S(1)} %get-tuple-element.773), channel_id=1, source_target_pairs={{0,1},{1,2},{2,3},{4,5},{5,6},{6,7},{8,9},{9,10},{10,11},{12,13},{... | collective-permute-start | bytes 12296 | tf_op jit(solution)/shard_map/while/body/eval_jaxpr/while/body/eval_jaxpr/ppermute | solution.py:21
  36.2 6.5 %collective-permute-start.5 = (f32[16,1024]{1,0:T(8,128)S(1)}, f32[16,1024]{1,0:T(8,128)S(1)}, u32[]{:S(2)}, u32[]{:S(2)}) collective-permute-start(f32[16,1024]{1,0:T(8,128)S(1)} %slice_bitcast_fusion.2), channel_id=1, source_target_pairs={{0,4},{4,8},{8,12},{12,16},{16,20},{20,24},{24,28},{1,5},{5,9},{9,... | collective-permute-start | bytes 196616 | tf_op jit(solution)/shard_map/while/body/eval_jaxpr/ppermute | solution.py:30
  45.1 5.5 %collective-permute-start.4 = (f32[1,1024]{1,0:T(1,128)S(1)}, f32[1,1024]{1,0:T(1,128)S(1)}, u32[]{:S(2)}, u32[]{:S(2)}) collective-permute-start(f32[1,1024]{1,0:T(1,128)S(1)} %get-tuple-element.773), channel_id=1, source_target_pairs={{0,1},{1,2},{2,3},{4,5},{5,6},{6,7},{8,9},{9,10},{10,11},{12,13},{... | collective-permute-start | bytes 12296 | tf_op jit(solution)/shard_map/while/body/eval_jaxpr/while/body/eval_jaxpr/ppermute | solution.py:21
  52.8 5.5 %collective-permute-start.4 = (f32[1,1024]{1,0:T(1,128)S(1)}, f32[1,1024]{1,0:T(1,128)S(1)}, u32[]{:S(2)}, u32[]{:S(2)}) collective-permute-start(f32[1,1024]{1,0:T(1,128)S(1)} %get-tuple-element.773), channel_id=1, source_target_pairs={{0,1},{1,2},{2,3},{4,5},{5,6},{6,7},{8,9},{9,10},{10,11},{12,13},{... | collective-permute-start | bytes 12296 | tf_op jit(solution)/shard_map/while/body/eval_jaxpr/while/body/eval_jaxpr/ppermute | solution.py:21
  59.1 6.5 %collective-permute-start.5 = (f32[16,1024]{1,0:T(8,128)S(1)}, f32[16,1024]{1,0:T(8,128)S(1)}, u32[]{:S(2)}, u32[]{:S(2)}) collective-permute-start(f32[16,1024]{1,0:T(8,128)S(1)} %slice_bitcast_fusion.2), channel_id=1, source_target_pairs={{0,4},{4,8},{8,12},{12,16},{16,20},{20,24},{24,28},{1,5},{5,9},{9,... | collective-permute-start | bytes 196616 | tf_op jit(solution)/shard_map/while/body/eval_jaxpr/ppermute | solution.py:30
  67.6 5.5 %collective-permute-start.4 = (f32[1,1024]{1,0:T(1,128)S(1)}, f32[1,1024]{1,0:T(1,128)S(1)}, u32[]{:S(2)}, u32[]{:S(2)}) collective-permute-start(f32[1,1024]{1,0:T(1,128)S(1)} %get-tuple-element.773), channel_id=1, source_target_pairs={{0,1},{1,2},{2,3},{4,5},{5,6},{6,7},{8,9},{9,10},{10,11},{12,13},{... | collective-permute-start | bytes 12296 | tf_op jit(solution)/shard_map/while/body/eval_jaxpr/while/body/eval_jaxpr/ppermute | solution.py:21
  75.3 5.5 %collective-permute-start.4 = (f32[1,1024]{1,0:T(1,128)S(1)}, f32[1,1024]{1,0:T(1,128)S(1)}, u32[]{:S(2)}, u32[]{:S(2)}) collective-permute-start(f32[1,1024]{1,0:T(1,128)S(1)} %get-tuple-element.773), channel_id=1, source_target_pairs={{0,1},{1,2},{2,3},{4,5},{5,6},{6,7},{8,9},{9,10},{10,11},{12,13},{... | collective-permute-start | bytes 12296 | tf_op jit(solution)/shard_map/while/body/eval_jaxpr/while/body/eval_jaxpr/ppermute | solution.py:21
  81.6 6.5 %collective-permute-start.5 = (f32[16,1024]{1,0:T(8,128)S(1)}, f32[16,1024]{1,0:T(8,128)S(1)}, u32[]{:S(2)}, u32[]{:S(2)}) collective-permute-start(f32[16,1024]{1,0:T(8,128)S(1)} %slice_bitcast_fusion.2), channel_id=1, source_target_pairs={{0,4},{4,8},{8,12},{12,16},{16,20},{20,24},{24,28},{1,5},{5,9},{9,... | collective-permute-start | bytes 196616 | tf_op jit(solution)/shard_map/while/body/eval_jaxpr/ppermute | solution.py:30
  90.1 5.5 %collective-permute-start.4 = (f32[1,1024]{1,0:T(1,128)S(1)}, f32[1,1024]{1,0:T(1,128)S(1)}, u32[]{:S(2)}, u32[]{:S(2)}) collective-permute-start(f32[1,1024]{1,0:T(1,128)S(1)} %get-tuple-element.773), channel_id=1, source_target_pairs={{0,1},{1,2},{2,3},{4,5},{5,6},{6,7},{8,9},{9,10},{10,11},{12,13},{... | collective-permute-start | bytes 12296 | tf_op jit(solution)/shard_map/while/body/eval_jaxpr/while/body/eval_jaxpr/ppermute | solution.py:21
  104.1 6.5 %collective-permute-start.5 = (f32[16,1024]{1,0:T(8,128)S(1)}, f32[16,1024]{1,0:T(8,128)S(1)}, u32[]{:S(2)}, u32[]{:S(2)}) collective-permute-start(f32[16,1024]{1,0:T(8,128)S(1)} %slice_bitcast_fusion.2), channel_id=1, source_target_pairs={{0,4},{4,8},{8,12},{12,16},{16,20},{20,24},{24,28},{1,5},{5,9},{9,... | collective-permute-start | bytes 196616 | tf_op jit(solution)/shard_map/while/body/eval_jaxpr/ppermute | solution.py:30
  126.6 6.5 %collective-permute-start.5 = (f32[16,1024]{1,0:T(8,128)S(1)}, f32[16,1024]{1,0:T(8,128)S(1)}, u32[]{:S(2)}, u32[]{:S(2)}) collective-permute-start(f32[16,1024]{1,0:T(8,128)S(1)} %slice_bitcast_fusion.2), channel_id=1, source_target_pairs={{0,4},{4,8},{8,12},{12,16},{16,20},{20,24},{24,28},{1,5},{5,9},{9,... | collective-permute-start | bytes 196616 | tf_op jit(solution)/shard_map/while/body/eval_jaxpr/ppermute | solution.py:30
  149.1 6.5 %collective-permute-start.5 = (f32[16,1024]{1,0:T(8,128)S(1)}, f32[16,1024]{1,0:T(8,128)S(1)}, u32[]{:S(2)}, u32[]{:S(2)}) collective-permute-start(f32[16,1024]{1,0:T(8,128)S(1)} %slice_bitcast_fusion.2), channel_id=1, source_target_pairs={{0,4},{4,8},{8,12},{12,16},{16,20},{20,24},{24,28},{1,5},{5,9},{9,... | collective-permute-start | bytes 196616 | tf_op jit(solution)/shard_map/while/body/eval_jaxpr/ppermute | solution.py:30
  171.6 6.5 %collective-permute-start.5 = (f32[16,1024]{1,0:T(8,128)S(1)}, f32[16,1024]{1,0:T(8,128)S(1)}, u32[]{:S(2)}, u32[]{:S(2)}) collective-permute-start(f32[16,1024]{1,0:T(8,128)S(1)} %slice_bitcast_fusion.2), channel_id=1, source_target_pairs={{0,4},{4,8},{8,12},{12,16},{16,20},{20,24},{24,28},{1,5},{5,9},{9,... | collective-permute-start | bytes 196616 | tf_op jit(solution)/shard_map/while/body/eval_jaxpr/ppermute | solution.py:30
  194.1 12.0 %collective-permute-start.6 = (f32[1,16,1024]{2,1,0:T(8,128)S(1)}, f32[1,16,1024]{2,1,0:T(8,128)S(1)}, u32[]{:S(2)}, u32[]{:S(2)}) collective-permute-start(f32[1,16,1024]{2,1,0:T(8,128)S(1)} %get-tuple-element.572), channel_id=1, source_target_pairs={{0,4},{4,8},{8,12},{12,16},{16,20},{20,24},{24,28},{1,5},{5,9},{9,... | collective-permute-start | bytes 196616 | tf_op jit(solution)/shard_map/ppermute | solution.py:21
  196.0 10.1 %collective-permute-start.7 = (f32[1,16,1024]{2,1,0:T(8,128)S(1)}, f32[1,16,1024]{2,1,0:T(8,128)S(1)}, u32[]{:S(2)}, u32[]{:S(2)}) collective-permute-start(f32[1,16,1024]{2,1,0:T(8,128)S(1)} %get-tuple-element.573), channel_id=1, source_target_pairs={{4,0},{8,4},{12,8},{16,12},{20,16},{24,20},{28,24},{5,1},{9,5},{13... | collective-permute-start | bytes 196616 | tf_op jit(solution)/shard_map/ppermute | solution.py:22
  206.2 12.0 %collective-permute-start.8 = (f32[4,1,1024]{2,1,0:T(1,128)S(1)}, f32[4,1,1024]{2,1,0:T(1,128)S(1)}, u32[]{:S(2)}, u32[]{:S(2)}) collective-permute-start(f32[4,1,1024]{2,1,0:T(1,128)S(1)} %get-tuple-element.570), channel_id=1, source_target_pairs={{0,1},{1,2},{2,3},{4,5},{5,6},{6,7},{8,9},{9,10},{10,11},{12,13},{... | collective-permute-start | bytes 49160 | tf_op jit(solution)/shard_map/ppermute | solution.py:21
  207.5 10.7 %collective-permute-start.9 = (f32[4,1,1024]{2,1,0:T(1,128)S(1)}, f32[4,1,1024]{2,1,0:T(1,128)S(1)}, u32[]{:S(2)}, u32[]{:S(2)}) collective-permute-start(f32[4,1,1024]{2,1,0:T(1,128)S(1)} %get-tuple-element.571), channel_id=1, source_target_pairs={{1,0},{2,1},{3,2},{5,4},{6,5},{7,6},{9,8},{10,9},{11,10},{13,12},{... | collective-permute-start | bytes 49160 | tf_op jit(solution)/shard_map/ppermute | solution.py:22
  212.1 6.9 %collective-permute-start.12 = (f32[6,4,1,1024]{3,0,2,1:T(8,128)S(1)}, f32[6,4,1,1024]{3,0,2,1:T(8,128)S(1)}, u32[]{:S(2)}, u32[]{:S(2)}) collective-permute-start(f32[6,4,1,1024]{3,0,2,1:T(8,128)S(1)} %get-tuple-element.566), channel_id=1, source_target_pairs={{0,1},{1,2},{2,3},{4,5},{5,6},{6,7},{8,9},{9,10},{10,11},{12,13},{... | collective-permute-start | bytes 294920 | tf_op jit(solution)/shard_map/ppermute | solution.py:21
  213.4 7.1 %collective-permute-start.13 = (f32[6,4,1,1024]{3,0,2,1:T(8,128)S(1)}, f32[6,4,1,1024]{3,0,2,1:T(8,128)S(1)}, u32[]{:S(2)}, u32[]{:S(2)}) collective-permute-start(f32[6,4,1,1024]{3,0,2,1:T(8,128)S(1)} %get-tuple-element.567), channel_id=1, source_target_pairs={{1,0},{2,1},{3,2},{5,4},{6,5},{7,6},{9,8},{10,9},{11,10},{13,12},{... | collective-permute-start | bytes 294920 | tf_op jit(solution)/shard_map/ppermute | solution.py:22
  297.4 5.7 %collective-permute-start = (f32[1,1024]{1,0:T(1,128)S(1)}, f32[1,1024]{1,0:T(1,128)S(1)}, u32[]{:S(2)}, u32[]{:S(2)}) collective-permute-start(f32[1,1024]{1,0:T(1,128)S(1)} %get-tuple-element.763), channel_id=1, source_target_pairs={{1,0},{2,1},{3,2},{5,4},{6,5},{7,6},{9,8},{10,9},{11,10},{13,12},{... | collective-permute-start | bytes 12296 | tf_op jit(solution)/shard_map/while/body/eval_jaxpr/while/body/eval_jaxpr/ppermute | solution.py:22
  (86 other events, 682.8 us)
where the time goes:
time: 462 us; the launch traced here: 457 us
  waiting for transfers between devices  190 us (41%)
  starting transfers between devices  165 us (36%)
  matrix products  70 us (15%)
  local copies, waits for them, and re-layouts  20.1 us (4%)
  other arithmetic  7.96 us (2%)
    ppermute x36, waiting for transfers between devices, extended(): before = lax.ppermute(last, axis, up)  135 us
    ppermute x36, starting transfers between devices, extended(): after = lax.ppermute(initial, axis, down)  85.7 us
    dot_general x54, matrix products, apply_blocks(): jnp.einsum('cd,dzxy->czxy', matrix, shifted, precision=highest)  69.8 us
    ppermute x16, waiting for transfers between devices, from_behind(): return lax.ppermute(block, axis, route)  53.4 us
    ppermute x36, starting transfers between devices, extended(): before = lax.ppermute(last, axis, up)  47.8 us
    ppermute x16, starting transfers between devices, from_behind(): return lax.ppermute(block, axis, route)  31.2 us
    while x40, local copies, waits for them, and re-layouts  10.2 us
  transfers between devices with their start and end apart: 88, of which 50 were waited for; matrix products, arithmetic and copies ran while one was open for 2% of the time, Pallas kernels for 0%

commit v1 on v0

v1 whole, which is shorter than its diff:
```python
import functools

import jax
import jax.numpy as jnp
import numpy as np
from jax import lax
from jax.experimental import pallas as pl
from jax.experimental.pallas import tpu as pltpu
from jax.sharding import PartitionSpec as P

smooth_eps = 0.0001
root_eps = 0.01
base_floor = 0.05
modulus_floor = 0.001
HALO = 8
MESH = pl.DeviceIdType.MESH
COPIES = 23
NO_KEY = 1 << 20


def lane_keys(layers, rows, first_field):
    deep = layers + 2
    inner = 3 * deep * rows
    total = inner + 2 * deep * HALO
    place = np.full((2, total), NO_KEY, np.int32)
    for k in range(total):
        if k < inner:
            place[0, k] = k // rows
            place[1, k] = k % rows
        else:
            e = k - inner
            side, z, f = e // (deep * HALO), (e // HALO) % deep, e % HALO - first_field
            if 0 <= f < 3:
                place[0, k] = f * deep + z
                place[1, k] = -1 if side == 0 else rows
    return place


def kernel(
    nb, nlat,
    pattern, blocks, keys, den, smask, disp, adj,
    force, sens,
    dext, rin, pext, sext, above, cbin, pas, base, coef, gext, dz, az, es, er,
    mats, xs, prod, send_sem, recv_sem,
):
    nl, nx, ny = den.shape
    rows = nx + 2 * HALO
    deep = nl + 2
    mid = slice(HALO, HALO + nx)
    lo = slice(0, HALO)
    hi = slice(HALO + nx, rows)
    b = lax.axis_index("build")
    l = lax.axis_index("lat")
    first_b, last_b = b == 0, b == nb - 1
    upper = b >= nb // 2

    top = nl - 1
    table = [
        (lambda: den.at[:, nx - HALO : nx], lambda: dext.at[:, lo], 0, 1),
        (lambda: den.at[:, 0:HALO], lambda: dext.at[:, hi], 0, -1),
        (lambda: es.at[1], lambda: er.at[0, 1 : 1 + nl], 0, 1),
        (lambda: es.at[0], lambda: er.at[1, 1 : 1 + nl], 0, -1),
        (lambda: es.at[1, top], lambda: er.at[0, 0], 1, 1),
        (lambda: es.at[0, top], lambda: er.at[1, 0], 1, -1),
        (lambda: es.at[1, 0], lambda: er.at[0, nl + 1], -1, 1),
        (lambda: es.at[0, 0], lambda: er.at[1, nl + 1], -1, -1),
        (lambda: adj.at[:, top], lambda: az.at[0], 1, 0),
        (lambda: adj.at[:, 0], lambda: az.at[1], -1, 0),
        (lambda: disp.at[:, top], lambda: dz.at[0], 1, 0),
        (lambda: disp.at[:, 0], lambda: dz.at[1], -1, 0),
        (lambda: pext.at[top, mid], lambda: rin.at[mid], 1, 0),
        (lambda: pext.at[top, nx : nx + HALO], lambda: rin.at[lo], 1, 1),
        (lambda: pext.at[top, HALO : 2 * HALO], lambda: rin.at[hi], 1, -1),
        (lambda: base.at[nx - HALO : nx], lambda: rin.at[lo], 0, 1),
        (lambda: base.at[0:HALO], lambda: rin.at[hi], 0, -1),
        (lambda: pext.at[0], lambda: above, -1, 0),
        (lambda: gext.at[:, nx : nx + HALO], lambda: gext.at[:, lo], 0, 1),
        (lambda: gext.at[:, HALO : 2 * HALO], lambda: gext.at[:, hi], 0, -1),
        (lambda: pas.at[0:nx], lambda: cbin.at[mid], -1, 0),
        (lambda: pas.at[nx - HALO : nx], lambda: cbin.at[lo], -1, 1),
        (lambda: pas.at[0:HALO], lambda: cbin.at[hi], -1, -1),
    ]

    def there(db, dl):
        ok = None
        for at, step, count in ((b, db, nb), (l, dl, nlat)):
            if step == 0:
                continue
            here = at < count - 1 if step > 0 else at > 0
            ok = here if ok is None else jnp.logical_and(ok, here)
        return ok

    def may_send(i):
        _, _, db, dl = table[i]
        ok = there(db, dl)
        return jnp.logical_and(ok, first_b) if i in (15, 16) else ok

    def may_take(i):
        _, _, db, dl = table[i]
        ok = there(-db, -dl)
        return jnp.logical_and(ok, first_b) if i in (15, 16) else ok

    def made(i):
        src, dst, db, dl = table[i]
        return pltpu.make_async_remote_copy(
            src_ref=src(), dst_ref=dst(),
            send_sem=send_sem.at[i], recv_sem=recv_sem.at[i],
            device_id=(b + db, l + dl), device_id_type=MESH,
        )

    def start(*numbers):
        for i in numbers:
            @pl.when(may_send(i))
            def _():
                made(i).start()

    def take(*numbers):
        for i in numbers:
            @pl.when(may_take(i))
            def _():
                made(i).wait_recv()

    def zero_if(cond, ref):
        @pl.when(cond)
        def _():
            ref[...] = jnp.zeros(ref.shape, jnp.float32)

    row_at = l * nx - HALO + lax.broadcasted_iota(jnp.int32, (rows, ny), 0)
    inside = jnp.logical_and(row_at >= 0, row_at < nlat * nx)

    def beside(w):
        col = lax.broadcasted_iota(jnp.int32, w.shape, 1)
        left = jnp.where(col == 0, 0.0, pltpu.roll(w, 1, 1))
        right = jnp.where(col == ny - 1, 0.0, pltpu.roll(w, ny - 1, 1))
        return left, right

    def cross(w):
        left, right = beside(w)
        return w + pltpu.roll(w, 1, 0) + pltpu.roll(w, rows - 1, 0) + left + right

    barrier = pltpu.get_barrier_semaphore()
    steps = [(i, j) for i in (-1, 0, 1) for j in (-1, 0, 1) if (i, j) != (0, 0)]
    for i, j in steps:
        @pl.when(there(i, j))
        def _():
            pl.semaphore_signal(barrier, inc=1, device_id=(b + i, l + j), device_id_type=MESH)
    wide = 1 + (b > 0).astype(jnp.int32) + (b < nb - 1).astype(jnp.int32)
    tall = 1 + (l > 0).astype(jnp.int32) + (l < nlat - 1).astype(jnp.int32)
    pl.semaphore_wait(barrier, wide * tall - 1)

    start(0, 1)

    @pl.when(first_b)
    def _():
        plane = base_floor + (1.0 - base_floor) * smask[...].astype(jnp.float32)
        base[...] = plane
        rin[mid] = plane

    start(15, 16)
    for z in range(nl):
        dext[z, mid] = den[z]
    for side, row in ((0, 0), (1, nx - 1)):
        for z in range(nl):
            for d in range(3):
                es[side, z, d : d + 1, :] = disp[d, z, row : row + 1, :]
                es[side, z, 3 + d : 4 + d, :] = adj[d, z, row : row + 1, :]
            es[side, z, 6:8, :] = jnp.zeros((2, ny), jnp.float32)
    start(2, 3, 4, 5, 6, 7, 8, 9)

    for i in (0, 1, 2, 3, 4, 5, 6, 7, 8, 9, 10, 11, 17, 18, 19, 20):
        _, dst, db, dl = table[i]
        zero_if(jnp.logical_not(there(-db, -dl)), dst())
    zero_if(l == 0, rin.at[lo])
    zero_if(l == nlat - 1, rin.at[hi])
    zero_if(jnp.logical_or(last_b, l == 0), cbin.at[lo])
    zero_if(jnp.logical_or(last_b, l == nlat - 1), cbin.at[hi])

    def forward():
        take(0, 1, 12, 13, 14, 15, 16)
        p = rin[...]
        for z in range(nl):
            p2 = p * p
            p4 = p2 * p2
            p8 = p4 * p4
            w = jnp.where(inside, p8 * p8, 0.0)
            total = jnp.where(inside, cross(w), 1.0)
            s = lax.rsqrt(lax.rsqrt(lax.rsqrt(lax.rsqrt(total))))
            d = dext[z]
            differ = d - s
            t = differ * differ + smooth_eps
            p = 0.5 * (d + s - t * lax.rsqrt(t) + root_eps)
            pext[z] = p
            sext[z] = s
        start(12, 13, 14, 17, 10, 11)
        for z in range(nl):
            p, s, d = pext[z], sext[z], dext[z]
            differ = d - s
            slope = differ * lax.rsqrt(differ * differ + smooth_eps)
            p2 = p * p
            p4 = p2 * p2
            p8 = p4 * p4
            s2 = s * s
            s4 = s2 * s2
            s8 = s4 * s4
            coef[0, z] = p8 * p4 * (p2 * p)
            coef[1, z] = jnp.where(inside, 0.5 * (1.0 + slope) / (s8 * s4 * (s2 * s)), 0.0)
            coef[2, z] = 0.5 * (1.0 - slope)
            coef[3, z] = (3.0 * (1.0 - modulus_floor)) * p2

    wide_k = keys.shape[-1]

    def build(which):
        x = lax.broadcasted_iota(jnp.int32, (nx, wide_k), 0)
        dzk = jnp.broadcast_to(keys[which, 0:1, :], (nx, wide_k))
        off = jnp.broadcast_to(keys[which, 1:2, :], (nx, wide_k)) - x + 1
        near = jnp.logical_and(off >= 0, off <= 2)
        key = jnp.where(near, dzk * 4 + off, -1)
        for z in range(nl):
            for c in range(3):
                sums = [jnp.zeros((nx, wide_k), jnp.float32) for _ in range(3)]
                for d in range(3):
                    for a in range(3):
                        for bx in range(3):
                            hit = key == (d * deep + z + a) * 4 + bx
                            for s in range(3):
                                o = 9 * a + 3 * bx + s
                                if which == 0:
                                    value = blocks[pattern[o], c, d]
                                else:
                                    value = blocks[pattern[26 - o], d, c]
                                sums[s] = jnp.where(hit, value, sums[s])
                for s in range(3):
                    at = ((s * 3 + c) * nl + z) * nx
                    high = sums[s].astype(jnp.bfloat16)
                    mats[0, at : at + nx, :] = high
                    mats[1, at : at + nx, :] = (sums[s] - high.astype(jnp.float32)).astype(
                        jnp.bfloat16
                    )

    def multiply():
        step = 256 if ny % 256 == 0 else 128

        def chunk(n, _):
            cols = pl.ds(pl.multiple_of(n * step, step), step)
            x = xs[:, cols]
            xh = x.astype(jnp.bfloat16)
            xl = (x - xh.astype(jnp.float32)).astype(jnp.bfloat16)
            dot = functools.partial(jnp.dot, preferred_element_type=jnp.float32)
            prod[:, cols] = dot(mats[0], xh) + (dot(mats[0], xl) + dot(mats[1], xh))
            return 0

        lax.fori_loop(0, ny // step, chunk, 0)

    def gathered(c):
        n = nl * nx
        left, _ = beside(prod[c * n : (c + 1) * n, :])
        _, right = beside(prod[(6 + c) * n : (7 + c) * n, :])
        return prod[(3 + c) * n : (4 + c) * n, :] + left + right

    inner = 3 * deep * nx

    def early():
        build(1)
        take(2, 3, 4, 5, 6, 7, 8, 9)
        for d in range(3):
            for z in range(deep):
                at = (d * deep + z) * nx
                if z == 0:
                    xs[at : at + nx, :] = az[0, d]
                elif z == deep - 1:
                    xs[at : at + nx, :] = az[1, d]
                else:
                    xs[at : at + nx, :] = adj[d, z - 1]
        for side in range(2):
            for z in range(deep):
                at = inner + (side * deep + z) * HALO
                xs[at : at + HALO, :] = er[side, z]
        multiply()
        parts = [gathered(c) for c in range(3)]
        for z in range(nl):
            g = disp[0, z] * parts[0][z * nx : (z + 1) * nx]
            g = g + disp[1, z] * parts[1][z * nx : (z + 1) * nx]
            gext[z, mid] = g + disp[2, z] * parts[2][z * nx : (z + 1) * nx]
        start(18, 19)
        build(0)

    def first(i, _):
        turn = (i == 0) == upper
        pl.when(turn)(early)
        pl.when(jnp.logical_not(turn))(forward)
        return 0

    lax.fori_loop(0, 2, first, 0)

    take(18, 19)
    for z in range(nl):
        coef[3, z] = coef[3, z] * gext[z]

    def stiffness():
        take(10, 11, 17)
        for z in range(deep):
            ref = rin if z == 0 else (above if z == deep - 1 else pext.at[z - 1])
            p = ref[mid]
            m = modulus_floor + (1.0 - modulus_floor) * (p * p * p)
            for d in range(3):
                at = (d * deep + z) * nx
                if z == 0:
                    u = dz[0, d]
                elif z == deep - 1:
                    u = dz[1, d]
                else:
                    u = disp[d, z - 1]
                xs[at : at + nx, :] = m * u
            for side, row in ((0, HALO - 1), (1, HALO + nx)):
                at = inner + (side * deep + z) * HALO
                p = ref[row : row + 1, :]
                m = modulus_floor + (1.0 - modulus_floor) * (p * p * p)
                xs[at : at + HALO, :] = m * er[side, z]
        multiply()
        for c in range(3):
            part = gathered(c)
            for z in range(nl):
                force[c, z] = part[z * nx : (z + 1) * nx]

    def backward():
        take(20, 21, 22)
        passed = cbin[...]
        for z in reversed(range(nl)):
            total = coef[3, z] + coef[0, z] * cross(passed)
            passed = total * coef[1, z]
            if z == 0:
                pas[...] = passed[HALO : HALO + nx]
                start(20, 21, 22)
            sens[z] = (total * coef[2, z])[HALO : HALO + nx]

    def second(i, _):
        turn = (i == 0) == upper
        pl.when(turn)(backward)
        pl.when(jnp.logical_not(turn))(stiffness)
        return 0

    lax.fori_loop(0, 2, second, 0)

    for i in range(COPIES):
        @pl.when(may_send(i))
        def _():
            made(i).wait_send()


def on_device(density, support_mask, pattern, blocks, displacement, adjoint):
    nb, nlat = lax.axis_size("build"), lax.axis_size("lat")
    nl, nx, ny = density.shape
    rows, deep = nx + 2 * HALO, nl + 2
    keys = np.stack([lane_keys(nl, nx, 0), lane_keys(nl, nx, 3)])
    wide_k = keys.shape[-1]
    f32 = jnp.float32
    vmem = pl.BlockSpec(memory_space=pltpu.VMEM)
    smem = pl.BlockSpec(memory_space=pltpu.SMEM)
    force, sens = pl.pallas_call(
        functools.partial(kernel, nb, nlat),
        out_shape=(
            jax.ShapeDtypeStruct(displacement.shape, f32),
            jax.ShapeDtypeStruct(density.shape, f32),
        ),
        in_specs=[smem, smem, vmem, vmem, vmem, vmem, vmem],
        out_specs=(vmem, vmem),
        scratch_shapes=[
            pltpu.VMEM((nl, rows, ny), f32),
            pltpu.VMEM((rows, ny), f32),
            pltpu.VMEM((nl, rows, ny), f32),
            pltpu.VMEM((nl, rows, ny), f32),
            pltpu.VMEM((rows, ny), f32),
            pltpu.VMEM((rows, ny), f32),
            pltpu.VMEM((nx, ny), f32),
            pltpu.VMEM((nx, ny), f32),
            pltpu.VMEM((4, nl, rows, ny), f32),
            pltpu.VMEM((nl, rows, ny), f32),
            pltpu.VMEM((2, 3, nx, ny), f32),
            pltpu.VMEM((2, 3, nx, ny), f32),
            pltpu.VMEM((2, nl, HALO, ny), f32),
            pltpu.VMEM((2, deep, HALO, ny), f32),
            pltpu.VMEM((2, 9 * nl * nx, wide_k), jnp.bfloat16),
            pltpu.VMEM((wide_k, ny), f32),
            pltpu.VMEM((9 * nl * nx, ny), f32),
            pltpu.SemaphoreType.DMA((COPIES,)),
            pltpu.SemaphoreType.DMA((COPIES,)),
        ],
        compiler_params=pltpu.CompilerParams(
            collective_id=0, has_side_effects=True, vmem_limit_bytes=48 * 1024 * 1024
        ),
    )(pattern, blocks, jnp.asarray(keys), density, support_mask, displacement, adjoint)
    return force, sens


def solution(mesh):
    in_specs = (
        P("build", "lat", None),
        P("lat", None),
        P(),
        P(),
        P(None, "build", "lat", None),
        P(None, "build", "lat", None),
    )
    out_specs = (P(None, "build", "lat", None), P("build", "lat", None))
    return jax.shard_map(
        on_device, mesh=mesh, in_specs=in_specs, out_specs=out_specs, check_vma=False
    )
```

time: 462 us -> 65.3 us (0.14)
  the two profiles are of different devices: /device:TPU:28 before, /device:TPU:0 now
where the time goes in v1:
time: 65.3 us; the launch traced here: 65 us
  Pallas kernels  58.4 us (89%)
  local copies, waits for them, and re-layouts  5.94 us (9%)
  between operations  0.66 us (1%)
    pallas_call x1, Pallas kernels, on_device(): pl.pallas_call(functools.partial(kernel, nb, nlat), out_shape=(jax.ShapeD...  58.4 us
    unnamed x15, local copies, waits for them, and re-layouts  5.94 us

profile of v1, /device:TPU:0, one launch (start us, length us, event | category | flops | bytes accessed | tf_op | source)
XLA Modules:
  0.0 65.0 jit_solution(15048226187605726169)
XLA Ops:
  0.6 0.0 copy-start.4
  0.6 0.0 copy-start.5
  0.7 0.8 %copy.9.blocks = f32[8,3,3]{2,1,0:T(4,128)S(1)} copy(f32[8,3,3]{0,2,1:T(4,128)} %param.10) | data formatting | bytes 576 | tf_op args[3]
  1.4 0.0 copy-done.4
  1.5 0.0 copy-done.5
  1.5 0.0 copy-start
  1.5 1.0 %copy-done = f32[3,2,16,1024]{3,2,1,0:T(8,128)S(1)} copy-done((f32[3,2,16,1024]{3,2,1,0:T(8,128)S(1)}, f32[3,2,16,1024]{3,2,1,0:T(8,128)}, u32[]{:S(2)}) %copy-start) | copy-done | bytes 393240
  2.5 0.0 copy-start.1
  2.5 1.0 %copy-done.1 = f32[3,2,16,1024]{3,2,1,0:T(8,128)S(1)} copy-done((f32[3,2,16,1024]{3,2,1,0:T(8,128)S(1)}, f32[3,2,16,1024]{3,2,1,0:T(8,128)}, u32[]{:S(2)}) %copy-start.1) | copy-done | bytes 393240
  3.4 0.0 copy-start.2
  3.5 0.9 %copy-done.2 = f32[2,16,1024]{2,1,0:T(8,128)S(1)} copy-done((f32[2,16,1024]{2,1,0:T(8,128)S(1)}, f32[2,16,1024]{2,1,0:T(8,128)}, u32[]{:S(2)}) %copy-start.2) | copy-done | bytes 131096
  4.4 0.0 copy-start.3
  4.4 0.8 %copy-done.3 = s32[16,1024]{1,0:T(8,128)S(1)} copy-done((s32[16,1024]{1,0:T(8,128)S(1)}, s32[16,1024]{1,0:T(8,128)}, u32[]{:S(2)}) %copy-start.3) | copy-done | bytes 65560
  5.2 58.4 %shard_map.86 = (f32[3,2,16,1024]{3,2,1,0:T(8,128)S(1)}, f32[2,16,1024]{2,1,0:T(8,128)S(1)}) custom-call(s32[27]{0:T(128)S(1)} %copy-done.5, f32[8,3,3]{2,1,0:T(4,128)S(1)} %copy.9.blocks, s32[2,2,256]{2,1,0:T(2,128)S(1)} %copy-done.4, f32[2,16,1024]{2,1,0:T(8,128)S(1)} %copy-done.2, s32[16,1024]{1,0:T(8,128)S(1)} %copy-done.3, ...), custom_call_target="tpu_custom_call" | custom-call | tf_op jit(solution)/shard_map/pallas_call | solution.py:359
  63.6 0.7 %copy.12 = f32[3,2,16,1024]{3,2,1,0:T(8,128)} copy(f32[3,2,16,1024]{3,2,1,0:T(8,128)S(1)} %get-tuple-element.4) | data formatting | bytes 786432
  64.3 0.7 %copy.13 = f32[2,16,1024]{2,1,0:T(8,128)} copy(f32[2,16,1024]{2,1,0:T(8,128)S(1)} %get-tuple-element.5) | data formatting | bytes 262144
Async XLA Ops:
  0.6 0.8 %copy-start.4 = (s32[2,2,256]{2,1,0:T(2,128)S(1)}, s32[2,2,256]{2,1,0:T(2,128)}, u32[]{:S(2)}) copy-start(s32[2,2,256]{2,1,0:T(2,128)} %constant.2.clone.keys) | copy-start | bytes 12292
  0.6 0.8 %copy-start.5 = (s32[27]{0:T(128)S(1)}, s32[27]{0:T(128)}, u32[]{:S(2)}) copy-start(s32[27]{0:T(128)} %pattern.1) | copy-start | bytes 328
  1.5 1.0 %copy-start = (f32[3,2,16,1024]{3,2,1,0:T(8,128)S(1)}, f32[3,2,16,1024]{3,2,1,0:T(8,128)}, u32[]{:S(2)}) copy-start(f32[3,2,16,1024]{3,2,1,0:T(8,128)} %disp.1) | copy-start | bytes 1179652
  2.5 1.0 %copy-start.1 = (f32[3,2,16,1024]{3,2,1,0:T(8,128)S(1)}, f32[3,2,16,1024]{3,2,1,0:T(8,128)}, u32[]{:S(2)}) copy-start(f32[3,2,16,1024]{3,2,1,0:T(8,128)} %adj.1) | copy-start | bytes 1179652
  3.4 0.9 %copy-start.2 = (f32[2,16,1024]{2,1,0:T(8,128)S(1)}, f32[2,16,1024]{2,1,0:T(8,128)}, u32[]{:S(2)}) copy-start(f32[2,16,1024]{2,1,0:T(8,128)} %den.1) | copy-start | bytes 393220
  4.4 0.8 %copy-start.3 = (s32[16,1024]{1,0:T(8,128)S(1)}, s32[16,1024]{1,0:T(8,128)}, u32[]{:S(2)}) copy-start(s32[16,1024]{1,0:T(8,128)} %smask.1) | copy-start | bytes 196612

commit v2 on v1

--- a/solution.py
+++ b/solution.py
@@ -38,10 +38,11 @@
 
 def kernel(
     nb, nlat,
-    pattern, blocks, keys, den, smask, disp, adj,
+    pattern, blocks, keys, den_in, smask_in, disp_in, adj_in,
     force, sens,
+    den, smask, disp, adj,
     dext, rin, pext, sext, above, cbin, pas, base, coef, gext, dz, az, es, er,
-    mats, xs, prod, send_sem, recv_sem,
+    mats, xs, prod, send_sem, recv_sem, local_sem,
 ):
     nl, nx, ny = den.shape
     rows = nx + 2 * HALO
@@ -138,6 +139,14 @@
         left, right = beside(w)
         return w + pltpu.roll(w, 1, 0) + pltpu.roll(w, rows - 1, 0) + left + right
 
+    loads = [
+        pltpu.make_async_copy(src, dst, local_sem.at[n])
+        for n, (src, dst) in enumerate(
+            ((den_in, den), (smask_in, smask), (adj_in, adj), (disp_in, disp))
+        )
+    ]
+    for load in loads:
+        load.start()
     barrier = pltpu.get_barrier_semaphore()
     steps = [(i, j) for i in (-1, 0, 1) for j in (-1, 0, 1) if (i, j) != (0, 0)]
     for i, j in steps:
@@ -148,7 +157,9 @@
     tall = 1 + (l > 0).astype(jnp.int32) + (l < nlat - 1).astype(jnp.int32)
     pl.semaphore_wait(barrier, wide * tall - 1)
 
+    loads[0].wait()
     start(0, 1)
+    loads[1].wait()
 
     @pl.when(first_b)
     def _():
@@ -159,6 +170,8 @@
     start(15, 16)
     for z in range(nl):
         dext[z, mid] = den[z]
+    loads[2].wait()
+    loads[3].wait()
     for side, row in ((0, 0), (1, nx - 1)):
         for z in range(nl):
             for d in range(3):
@@ -166,6 +179,10 @@
                 es[side, z, 3 + d : 4 + d, :] = adj[d, z, row : row + 1, :]
             es[side, z, 6:8, :] = jnp.zeros((2, ny), jnp.float32)
     start(2, 3, 4, 5, 6, 7, 8, 9)
+
+    @pl.when(upper)
+    def _():
+        start(10, 11)
 
     for i in (0, 1, 2, 3, 4, 5, 6, 7, 8, 9, 10, 11, 17, 18, 19, 20):
         _, dst, db, dl = table[i]
@@ -191,7 +208,7 @@
             p = 0.5 * (d + s - t * lax.rsqrt(t) + root_eps)
             pext[z] = p
             sext[z] = s
-        start(12, 13, 14, 17, 10, 11)
+        start(13, 14, 12, 17)
         for z in range(nl):
             p, s, d = pext[z], sext[z], dext[z]
             differ = d - s
@@ -225,9 +242,9 @@
                             for s in range(3):
                                 o = 9 * a + 3 * bx + s
                                 if which == 0:
-                                    value = blocks[pattern[o], c, d]
+                                    value = blocks[c, d, pattern[o]]
                                 else:
-                                    value = blocks[pattern[26 - o], d, c]
+                                    value = blocks[d, c, pattern[26 - o]]
                                 sums[s] = jnp.where(hit, value, sums[s])
                 for s in range(3):
                     at = ((s * 3 + c) * nl + z) * nx
@@ -291,6 +308,10 @@
         return 0
 
     lax.fori_loop(0, 2, first, 0)
+
+    @pl.when(jnp.logical_not(upper))
+    def _():
+        start(10, 11)
 
     take(18, 19)
     for z in range(nl):
@@ -330,7 +351,7 @@
             passed = total * coef[1, z]
             if z == 0:
                 pas[...] = passed[HALO : HALO + nx]
-                start(20, 21, 22)
+                start(21, 22, 20)
             sens[z] = (total * coef[2, z])[HALO : HALO + nx]
 
     def second(i, _):
@@ -356,15 +377,20 @@
     f32 = jnp.float32
     vmem = pl.BlockSpec(memory_space=pltpu.VMEM)
     smem = pl.BlockSpec(memory_space=pltpu.SMEM)
+    hbm = pl.BlockSpec(memory_space=pltpu.HBM)
     force, sens = pl.pallas_call(
         functools.partial(kernel, nb, nlat),
         out_shape=(
             jax.ShapeDtypeStruct(displacement.shape, f32),
             jax.ShapeDtypeStruct(density.shape, f32),
         ),
-        in_specs=[smem, smem, vmem, vmem, vmem, vmem, vmem],
+        in_specs=[smem, smem, vmem, hbm, hbm, hbm, hbm],
         out_specs=(vmem, vmem),
         scratch_shapes=[
+            pltpu.VMEM(density.shape, f32),
+            pltpu.VMEM(support_mask.shape, jnp.int32),
+            pltpu.VMEM(displacement.shape, f32),
+            pltpu.VMEM(adjoint.shape, f32),
             pltpu.VMEM((nl, rows, ny), f32),
             pltpu.VMEM((rows, ny), f32),
             pltpu.VMEM((nl, rows, ny), f32),
@@ -384,11 +410,12 @@
             pltpu.VMEM((9 * nl * nx, ny), f32),
             pltpu.SemaphoreType.DMA((COPIES,)),
             pltpu.SemaphoreType.DMA((COPIES,)),
+            pltpu.SemaphoreType.DMA((4,)),
         ],
         compiler_params=pltpu.CompilerParams(
-            collective_id=0, has_side_effects=True, vmem_limit_bytes=48 * 1024 * 1024
+            collective_id=0, has_side_effects=True, vmem_limit_bytes=63 * 1024 * 1024
         ),
-    )(pattern, blocks, jnp.asarray(keys), density, support_mask, displacement, adjoint)
+    )(pattern, jnp.transpose(blocks, (1, 2, 0)), jnp.asarray(keys), density, support_mask, displacement, adjoint)
     return force, sens
 
 

time: 65.3 us -> 62.4 us (0.956)
  local copies, waits for them, and re-layouts: 5.94 us -> 2.46 us
  Pallas kernels: 58.4 us -> 59.1 us
    unnamed x15 -> x4, local copies, waits for them, and re-layouts: 5.94 us -> 2.46 us
    pallas_call x1, Pallas kernels: 58.4 us -> 59.1 us  [on_device(): pl.pallas_call(functools.partial(kernel, nb, nlat), out_shape=(jax.ShapeD...]
where the time goes in v2:
time: 62.4 us; the launch traced here: 62.2 us
  Pallas kernels  59.1 us (95%)
  local copies, waits for them, and re-layouts  2.46 us (4%)
  between operations  0.65 us (1%)
    pallas_call x1, Pallas kernels, on_device(): pl.pallas_call(functools.partial(kernel, nb, nlat), out_shape=(jax.ShapeD...  59.1 us
    unnamed x4, local copies, waits for them, and re-layouts  2.46 us

profile of v2, /device:TPU:0, one launch (start us, length us, event | category | flops | bytes accessed | tf_op | source)
XLA Modules:
  0.0 62.2 jit_solution(15581481508783533687)
XLA Ops:
  0.6 59.1 %shard_map.86 = (f32[3,2,16,1024]{3,2,1,0:T(8,128)}, f32[2,16,1024]{2,1,0:T(8,128)}) custom-call(s32[27]{0:T(128)} %pattern.1, f32[3,3,8]{2,1,0:T(4,128)} %bitcast.1, s32[2,2,256]{2,1,0:T(2,128)} %constant.2.clone.keys, f32[2,16,1024]{2,1,0:T(8,128)} %den_in.1, s32[16,1024]{1,0:T(8,128)} %smask_in.1, f32[3,2,16,1024]{3,2,1,0:T(8,128)} %disp_in.1, ...), custom_call_target="tpu_custom_call" | custom-call | tf_op jit(solution)/shard_map/pallas_call | solution.py:381
  59.8 0.0 copy-start
  59.8 1.8 %copy.11 = f32[3,2,16,1024]{3,2,1,0:T(8,128)} copy(f32[3,2,16,1024]{3,2,1,0:T(8,128)} %get-tuple-element.4) | data formatting | bytes 786432
  61.6 0.0 copy-done
  61.6 0.7 %copy.12 = f32[2,16,1024]{2,1,0:T(8,128)} copy(f32[2,16,1024]{2,1,0:T(8,128)S(1)} %copy-done) | data formatting | bytes 262144
Async XLA Ops:
  59.8 1.8 %copy-start = (f32[2,16,1024]{2,1,0:T(8,128)S(1)}, f32[2,16,1024]{2,1,0:T(8,128)}, u32[]{:S(2)}) copy-start(f32[2,16,1024]{2,1,0:T(8,128)} %get-tuple-element.5) | copy-start | bytes 393220

commit v3 on v2

--- a/solution.py
+++ b/solution.py
@@ -14,7 +14,7 @@
 modulus_floor = 0.001
 HALO = 8
 MESH = pl.DeviceIdType.MESH
-COPIES = 23
+COPIES = 31
 NO_KEY = 1 << 20
 
 
@@ -36,12 +36,20 @@
     return place
 
 
+def column_frames(nb, nl, ny):
+    spare = 128 * (-(-nb * nl // 128))
+    half = ny // 2
+    if half % 128 or half <= spare:
+        return [(0, ny, 0, ny)]
+    return [(0, half + spare, 0, half), (half - spare, half + spare, half, ny)]
+
+
 def kernel(
     nb, nlat,
     pattern, blocks, keys, den_in, smask_in, disp_in, adj_in,
     force, sens,
     den, smask, disp, adj,
-    dext, rin, pext, sext, above, cbin, pas, base, coef, gext, dz, az, es, er,
+    dext, rin, below, pout, pext, sext, above, cbin, pas, base, coef, gext, dz, az, es, er,
     mats, xs, prod, send_sem, recv_sem, local_sem,
 ):
     nl, nx, ny = den.shape
@@ -56,6 +64,29 @@
     upper = b >= nb // 2
 
     top = nl - 1
+    frames = column_frames(nb, nl, ny)
+    edge = (15, 16, 26, 27)
+    up = ((13, 14, 12), (24, 25, 23))
+    down = ((21, 22, 20), (29, 30, 28))
+
+    def forward_copies(f):
+        start_col, width = frames[f][:2]
+        cols = slice(start_col, start_col + width)
+        return [
+            (lambda: pout.at[f, mid], lambda: rin.at[f, mid], 1, 0),
+            (lambda: pout.at[f, nx : nx + HALO], lambda: rin.at[f, lo], 1, 1),
+            (lambda: pout.at[f, HALO : 2 * HALO], lambda: rin.at[f, hi], 1, -1),
+            (lambda: base.at[nx - HALO : nx, cols], lambda: rin.at[f, lo], 0, 1),
+            (lambda: base.at[0:HALO, cols], lambda: rin.at[f, hi], 0, -1),
+        ]
+
+    def backward_copies(f):
+        return [
+            (lambda: pas.at[f, 0:nx], lambda: cbin.at[f, mid], -1, 0),
+            (lambda: pas.at[f, nx - HALO : nx], lambda: cbin.at[f, lo], -1, 1),
+            (lambda: pas.at[f, 0:HALO], lambda: cbin.at[f, hi], -1, -1),
+        ]
+
     table = [
         (lambda: den.at[:, nx - HALO : nx], lambda: dext.at[:, lo], 0, 1),
         (lambda: den.at[:, 0:HALO], lambda: dext.at[:, hi], 0, -1),
@@ -69,17 +100,13 @@
         (lambda: adj.at[:, 0], lambda: az.at[1], -1, 0),
         (lambda: disp.at[:, top], lambda: dz.at[0], 1, 0),
         (lambda: disp.at[:, 0], lambda: dz.at[1], -1, 0),
-        (lambda: pext.at[top, mid], lambda: rin.at[mid], 1, 0),
-        (lambda: pext.at[top, nx : nx + HALO], lambda: rin.at[lo], 1, 1),
-        (lambda: pext.at[top, HALO : 2 * HALO], lambda: rin.at[hi], 1, -1),
-        (lambda: base.at[nx - HALO : nx], lambda: rin.at[lo], 0, 1),
-        (lambda: base.at[0:HALO], lambda: rin.at[hi], 0, -1),
+        *forward_copies(0),
         (lambda: pext.at[0], lambda: above, -1, 0),
         (lambda: gext.at[:, nx : nx + HALO], lambda: gext.at[:, lo], 0, 1),
         (lambda: gext.at[:, HALO : 2 * HALO], lambda: gext.at[:, hi], 0, -1),
-        (lambda: pas.at[0:nx], lambda: cbin.at[mid], -1, 0),
-        (lambda: pas.at[nx - HALO : nx], lambda: cbin.at[lo], -1, 1),
-        (lambda: pas.at[0:HALO], lambda: cbin.at[hi], -1, -1),
+        *backward_copies(0),
+        *(forward_copies(1) if len(frames) == 2 else ()),
+        *(backward_copies(1) if len(frames) == 2 else ()),
     ]
 
     def there(db, dl):
@@ -94,12 +121,12 @@
     def may_send(i):
         _, _, db, dl = table[i]
         ok = there(db, dl)
-        return jnp.logical_and(ok, first_b) if i in (15, 16) else ok
+        return jnp.logical_and(ok, first_b) if i in edge else ok
 
     def may_take(i):
         _, _, db, dl = table[i]
         ok = there(-db, -dl)
-        return jnp.logical_and(ok, first_b) if i in (15, 16) else ok
+        return jnp.logical_and(ok, first_b) if i in edge else ok
 
     def made(i):
         src, dst, db, dl = table[i]
@@ -126,13 +153,14 @@
         def _():
             ref[...] = jnp.zeros(ref.shape, jnp.float32)
 
-    row_at = l * nx - HALO + lax.broadcasted_iota(jnp.int32, (rows, ny), 0)
-    inside = jnp.logical_and(row_at >= 0, row_at < nlat * nx)
+    def within(width):
+        row_at = l * nx - HALO + lax.broadcasted_iota(jnp.int32, (rows, width), 0)
+        return jnp.logical_and(row_at >= 0, row_at < nlat * nx)
 
     def beside(w):
         col = lax.broadcasted_iota(jnp.int32, w.shape, 1)
         left = jnp.where(col == 0, 0.0, pltpu.roll(w, 1, 1))
-        right = jnp.where(col == ny - 1, 0.0, pltpu.roll(w, ny - 1, 1))
+        right = jnp.where(col == w.shape[1] - 1, 0.0, pltpu.roll(w, w.shape[1] - 1, 1))
         return left, right
 
     def cross(w):
@@ -165,9 +193,10 @@
     def _():
         plane = base_floor + (1.0 - base_floor) * smask[...].astype(jnp.float32)
         base[...] = plane
-        rin[mid] = plane
-
-    start(15, 16)
+        for f, (start_col, width, *_) in enumerate(frames):
+            rin[f, mid] = plane[:, start_col : start_col + width]
+
+    start(*edge[: 2 * len(frames)])
     for z in range(nl):
         dext[z, mid] = den[z]
     loads[2].wait()
@@ -184,31 +213,42 @@
     def _():
         start(10, 11)
 
-    for i in (0, 1, 2, 3, 4, 5, 6, 7, 8, 9, 10, 11, 17, 18, 19, 20):
+    for i in (0, 1, 2, 3, 4, 5, 6, 7, 8, 9, 10, 11, 17, 18, 19):
         _, dst, db, dl = table[i]
         zero_if(jnp.logical_not(there(-db, -dl)), dst())
-    zero_if(l == 0, rin.at[lo])
-    zero_if(l == nlat - 1, rin.at[hi])
-    zero_if(jnp.logical_or(last_b, l == 0), cbin.at[lo])
-    zero_if(jnp.logical_or(last_b, l == nlat - 1), cbin.at[hi])
+    for f in range(len(frames)):
+        zero_if(l == 0, rin.at[f, lo])
+        zero_if(l == nlat - 1, rin.at[f, hi])
+        zero_if(last_b, cbin.at[f, mid])
+        zero_if(jnp.logical_or(last_b, l == 0), cbin.at[f, lo])
+        zero_if(jnp.logical_or(last_b, l == nlat - 1), cbin.at[f, hi])
 
     def forward():
-        take(0, 1, 12, 13, 14, 15, 16)
-        p = rin[...]
-        for z in range(nl):
-            p2 = p * p
-            p4 = p2 * p2
-            p8 = p4 * p4
-            w = jnp.where(inside, p8 * p8, 0.0)
-            total = jnp.where(inside, cross(w), 1.0)
-            s = lax.rsqrt(lax.rsqrt(lax.rsqrt(lax.rsqrt(total))))
-            d = dext[z]
-            differ = d - s
-            t = differ * differ + smooth_eps
-            p = 0.5 * (d + s - t * lax.rsqrt(t) + root_eps)
-            pext[z] = p
-            sext[z] = s
-        start(13, 14, 12, 17)
+        take(0, 1)
+        for f, (start_col, width, kept, until) in enumerate(frames):
+            own, inner_cols = slice(kept, until), slice(kept - start_col, until - start_col)
+            inside = within(width)
+            take(*up[f], *edge[2 * f : 2 * f + 2])
+            p = rin[f]
+            for z in range(nl):
+                p2 = p * p
+                p4 = p2 * p2
+                p8 = p4 * p4
+                w = jnp.where(inside, p8 * p8, 0.0)
+                total = jnp.where(inside, cross(w), 1.0)
+                s = lax.rsqrt(lax.rsqrt(lax.rsqrt(lax.rsqrt(total))))
+                d = dext[z, :, start_col : start_col + width]
+                differ = d - s
+                t = differ * differ + smooth_eps
+                p = 0.5 * (d + s - t * lax.rsqrt(t) + root_eps)
+                if z == top:
+                    pout[f] = p
+                    start(*up[f])
+                pext[z, :, own] = p[:, inner_cols]
+                sext[z, :, own] = s[:, inner_cols]
+            below[:, own] = rin[f, :, inner_cols]
+        start(17)
+        inside = within(ny)
         for z in range(nl):
             p, s, d = pext[z], sext[z], dext[z]
             differ = d - s
@@ -320,7 +360,7 @@
     def stiffness():
         take(10, 11, 17)
         for z in range(deep):
-            ref = rin if z == 0 else (above if z == deep - 1 else pext.at[z - 1])
+            ref = below if z == 0 else (above if z == deep - 1 else pext.at[z - 1])
             p = ref[mid]
             m = modulus_floor + (1.0 - modulus_floor) * (p * p * p)
             for d in range(3):
@@ -344,15 +384,18 @@
                 force[c, z] = part[z * nx : (z + 1) * nx]
 
     def backward():
-        take(20, 21, 22)
-        passed = cbin[...]
-        for z in reversed(range(nl)):
-            total = coef[3, z] + coef[0, z] * cross(passed)
-            passed = total * coef[1, z]
-            if z == 0:
-                pas[...] = passed[HALO : HALO + nx]
-                start(21, 22, 20)
-            sens[z] = (total * coef[2, z])[HALO : HALO + nx]
+        for f, (start_col, width, kept, until) in enumerate(frames):
+            cols = slice(start_col, start_col + width)
+            own, inner_cols = slice(kept, until), slice(kept - start_col, until - start_col)
+            take(*down[f])
+            passed = cbin[f]
+            for z in reversed(range(nl)):
+                total = coef[3, z, :, cols] + coef[0, z, :, cols] * cross(passed)
+                passed = total * coef[1, z, :, cols]
+                if z == 0:
+                    pas[f] = passed[mid]
+                    start(*down[f])
+                sens[z, :, own] = (total[:, inner_cols] * coef[2, z, :, own])[mid]
 
     def second(i, _):
         turn = (i == 0) == upper
@@ -362,7 +405,7 @@
 
     lax.fori_loop(0, 2, second, 0)
 
-    for i in range(COPIES):
+    for i in range(len(table)):
         @pl.when(may_send(i))
         def _():
             made(i).wait_send()
@@ -373,6 +416,8 @@
     nl, nx, ny = density.shape
     rows, deep = nx + 2 * HALO, nl + 2
     keys = np.stack([lane_keys(nl, nx, 0), lane_keys(nl, nx, 3)])
+    frames = column_frames(nb, nl, ny)
+    count, width = len(frames), frames[0][1]
     wide_k = keys.shape[-1]
     f32 = jnp.float32
     vmem = pl.BlockSpec(memory_space=pltpu.VMEM)
@@ -392,12 +437,14 @@
             pltpu.VMEM(displacement.shape, f32),
             pltpu.VMEM(adjoint.shape, f32),
             pltpu.VMEM((nl, rows, ny), f32),
+            pltpu.VMEM((count, rows, width), f32),
             pltpu.VMEM((rows, ny), f32),
+            pltpu.VMEM((count, rows, width), f32),
             pltpu.VMEM((nl, rows, ny), f32),
             pltpu.VMEM((nl, rows, ny), f32),
             pltpu.VMEM((rows, ny), f32),
-            pltpu.VMEM((rows, ny), f32),
-            pltpu.VMEM((nx, ny), f32),
+            pltpu.VMEM((count, rows, width), f32),
+            pltpu.VMEM((count, nx, width), f32),
             pltpu.VMEM((nx, ny), f32),
             pltpu.VMEM((4, nl, rows, ny), f32),
             pltpu.VMEM((nl, rows, ny), f32),

time: 62.4 us -> 59.6 us (0.955)
  Pallas kernels: 59.1 us -> 56.3 us
    pallas_call x1, Pallas kernels: 59.1 us -> 56.3 us  [on_device(): pl.pallas_call(functools.partial(kernel, nb, nlat), out_shape=(jax.ShapeD...]
where the time goes in v3:
time: 59.6 us; the launch traced here: 59.4 us
  Pallas kernels  56.3 us (94%)
  local copies, waits for them, and re-layouts  2.46 us (4%)
  between operations  0.65 us (1%)
    pallas_call x1, Pallas kernels, on_device(): pl.pallas_call(functools.partial(kernel, nb, nlat), out_shape=(jax.ShapeD...  56.3 us
    unnamed x4, local copies, waits for them, and re-layouts  2.46 us

profile of v3, /device:TPU:0, one launch (start us, length us, event | category | flops | bytes accessed | tf_op | source)
XLA Modules:
  0.0 59.4 jit_solution(17818917115339604949)
XLA Ops:
  0.6 56.3 %shard_map.86 = (f32[3,2,16,1024]{3,2,1,0:T(8,128)}, f32[2,16,1024]{2,1,0:T(8,128)}) custom-call(s32[27]{0:T(128)} %pattern.1, f32[3,3,8]{2,1,0:T(4,128)} %bitcast.1, s32[2,2,256]{2,1,0:T(2,128)} %constant.2.clone.keys, f32[2,16,1024]{2,1,0:T(8,128)} %den_in.1, s32[16,1024]{1,0:T(8,128)} %smask_in.1, f32[3,2,16,1024]{3,2,1,0:T(8,128)} %disp_in.1, ...), custom_call_target="tpu_custom_call" | custom-call | tf_op jit(solution)/shard_map/pallas_call | solution.py:426
  57.0 0.0 copy-start
  57.0 1.8 %copy.11 = f32[3,2,16,1024]{3,2,1,0:T(8,128)} copy(f32[3,2,16,1024]{3,2,1,0:T(8,128)} %get-tuple-element.4) | data formatting | bytes 786432
  58.8 0.0 copy-done
  58.8 0.7 %copy.12 = f32[2,16,1024]{2,1,0:T(8,128)} copy(f32[2,16,1024]{2,1,0:T(8,128)S(1)} %copy-done) | data formatting | bytes 262144
Async XLA Ops:
  57.0 1.8 %copy-start = (f32[2,16,1024]{2,1,0:T(8,128)S(1)}, f32[2,16,1024]{2,1,0:T(8,128)}, u32[]{:S(2)}) copy-start(f32[2,16,1024]{2,1,0:T(8,128)} %get-tuple-element.5) | copy-start | bytes 393220

commit v4 on v3

--- a/solution.py
+++ b/solution.py
@@ -199,29 +199,12 @@
     start(*edge[: 2 * len(frames)])
     for z in range(nl):
         dext[z, mid] = den[z]
-    loads[2].wait()
-    loads[3].wait()
-    for side, row in ((0, 0), (1, nx - 1)):
-        for z in range(nl):
-            for d in range(3):
-                es[side, z, d : d + 1, :] = disp[d, z, row : row + 1, :]
-                es[side, z, 3 + d : 4 + d, :] = adj[d, z, row : row + 1, :]
-            es[side, z, 6:8, :] = jnp.zeros((2, ny), jnp.float32)
-    start(2, 3, 4, 5, 6, 7, 8, 9)
-
-    @pl.when(upper)
-    def _():
-        start(10, 11)
-
-    for i in (0, 1, 2, 3, 4, 5, 6, 7, 8, 9, 10, 11, 17, 18, 19):
+    for i in (0, 1):
         _, dst, db, dl = table[i]
         zero_if(jnp.logical_not(there(-db, -dl)), dst())
     for f in range(len(frames)):
         zero_if(l == 0, rin.at[f, lo])
         zero_if(l == nlat - 1, rin.at[f, hi])
-        zero_if(last_b, cbin.at[f, mid])
-        zero_if(jnp.logical_or(last_b, l == 0), cbin.at[f, lo])
-        zero_if(jnp.logical_or(last_b, l == nlat - 1), cbin.at[f, hi])
 
     def forward():
         take(0, 1)
@@ -264,6 +247,30 @@
             coef[2, z] = 0.5 * (1.0 - slope)
             coef[3, z] = (3.0 * (1.0 - modulus_floor)) * p2
 
+    pl.when(first_b)(forward)
+
+    loads[2].wait()
+    loads[3].wait()
+    for side, row in ((0, 0), (1, nx - 1)):
+        for z in range(nl):
+            for d in range(3):
+                es[side, z, d : d + 1, :] = disp[d, z, row : row + 1, :]
+                es[side, z, 3 + d : 4 + d, :] = adj[d, z, row : row + 1, :]
+            es[side, z, 6:8, :] = jnp.zeros((2, ny), jnp.float32)
+    start(2, 3, 4, 5, 6, 7, 8, 9)
+
+    @pl.when(upper)
+    def _():
+        start(10, 11)
+
+    for i in (2, 3, 4, 5, 6, 7, 8, 9, 10, 11, 17, 18, 19):
+        _, dst, db, dl = table[i]
+        zero_if(jnp.logical_not(there(-db, -dl)), dst())
+    for f in range(len(frames)):
+        zero_if(last_b, cbin.at[f, mid])
+        zero_if(jnp.logical_or(last_b, l == 0), cbin.at[f, lo])
+        zero_if(jnp.logical_or(last_b, l == nlat - 1), cbin.at[f, hi])
+
     wide_k = keys.shape[-1]
 
     def build(which):
@@ -344,7 +351,7 @@
     def first(i, _):
         turn = (i == 0) == upper
         pl.when(turn)(early)
-        pl.when(jnp.logical_not(turn))(forward)
+        pl.when(jnp.logical_not(jnp.logical_or(turn, first_b)))(forward)
         return 0
 
     lax.fori_loop(0, 2, first, 0)

time: 59.6 us -> 59.8 us (level)
  no operation moved by 1% of the time
where the time goes in v4:
time: 59.8 us; the launch traced here: 59.6 us
  Pallas kernels  56.5 us (94%)
  local copies, waits for them, and re-layouts  2.46 us (4%)
  between operations  0.65 us (1%)
    pallas_call x1, Pallas kernels, on_device(): pl.pallas_call(functools.partial(kernel, nb, nlat), out_shape=(jax.ShapeD...  56.5 us
    unnamed x4, local copies, waits for them, and re-layouts  2.46 us

profile of v4, /device:TPU:0, one launch (start us, length us, event | category | flops | bytes accessed | tf_op | source)
XLA Modules:
  0.0 59.6 jit_solution(1942773900120799339)
XLA Ops:
  0.6 56.5 %shard_map.86 = (f32[3,2,16,1024]{3,2,1,0:T(8,128)}, f32[2,16,1024]{2,1,0:T(8,128)}) custom-call(s32[27]{0:T(128)} %pattern.1, f32[3,3,8]{2,1,0:T(4,128)} %bitcast.1, s32[2,2,256]{2,1,0:T(2,128)} %constant.2.clone.keys, f32[2,16,1024]{2,1,0:T(8,128)} %den_in.1, s32[16,1024]{1,0:T(8,128)} %smask_in.1, f32[3,2,16,1024]{3,2,1,0:T(8,128)} %disp_in.1, ...), custom_call_target="tpu_custom_call" | custom-call | tf_op jit(solution)/shard_map/pallas_call | solution.py:433
  57.1 0.0 copy-start
  57.1 1.8 %copy.11 = f32[3,2,16,1024]{3,2,1,0:T(8,128)} copy(f32[3,2,16,1024]{3,2,1,0:T(8,128)} %get-tuple-element.4) | data formatting | bytes 786432
  58.9 0.0 copy-done
  58.9 0.7 %copy.12 = f32[2,16,1024]{2,1,0:T(8,128)} copy(f32[2,16,1024]{2,1,0:T(8,128)S(1)} %copy-done) | data formatting | bytes 262144
Async XLA Ops:
  57.1 1.8 %copy-start = (f32[2,16,1024]{2,1,0:T(8,128)S(1)}, f32[2,16,1024]{2,1,0:T(8,128)}, u32[]{:S(2)}) copy-start(f32[2,16,1024]{2,1,0:T(8,128)} %get-tuple-element.5) | copy-start | bytes 393220
